TPU v7x, 1024 devices: a whole 8x8x8 slice. The times are simulated.
1024 devices in a mesh: wide: 128 (over y, z, core), narrow: 8 (over x).
Axes of the slice: x: 8, y: 8, z: 8, core: 2. Of those that a mesh axis runs over, the one named last changes fastest.
Arguments:
- tokens: bfloat16 [4096, 4096], P('wide', 'narrow'), may hold values from -6 to 6
- cotangent: bfloat16 [4096, 4096], P('wide', 'narrow'), may hold values from -6 to 6
- gate_logits: float32 [4096, 4], P('wide'), may hold values from -6 to 6
- node_groups: int32 [4096, 4], P('wide'), may hold values from 0 to 127, all different within a row; in each aligned block of 32 rows (0 to 31, 32 to 63, ...) at most 2 rows name the same one
- sample_ids: int32 [4096], P('wide'), may hold values from 0 to 63
- advantages: float32 [64], replicated, may hold values from -4 to 4
- up_weight: bfloat16 [128, 4096, 1024], P('wide', 'narrow'), may hold values from -0.09375 to 0.09375
- down_weight: bfloat16 [128, 1024, 4096], P('wide', None, 'narrow'), may hold values from -0.1875 to 0.1875
Outputs:
- mixed: bfloat16 [4096, 4096], P('wide', 'narrow')
- token_grad: bfloat16 [4096, 4096], P('wide', 'narrow')
- logit_grad: float32 [4096, 4], P('wide')
Inputs may be any that keep to these rules, and one draw needn't show every extreme that they name: `node_groups`: the 4 node groups of a token are distinct. Among the tokens of one index of wide (aligned blocks of 32 tokens), at most 2 name any one node group, and some node group is named by exactly 2 of them.
All inputs are finite; a program needn't handle non-finite values.
Results may differ from a plain program's by a relative error of at most 0.034.
Values may be sent and summed in bfloat16 or wider, within the bound.
A program may use at most 32 MiB of HBM per device.

v0:
```python
import jax
import jax.numpy as jnp
from jax import lax
from jax.sharding import PartitionSpec as P

route_scale = 2.5


def silu_slope(pre):
    sig = jax.nn.sigmoid(pre)
    return sig * (1.0 + pre * (1.0 - sig))


def shards(
    tokens, cotangent, gate_logits, node_groups, sample_ids, advantages, up_weight, down_weight
):
    tok_rows, feat = tokens.shape
    picks = node_groups.shape[1]
    groups = lax.axis_size("wide")
    slots = max(2, 6 * tok_rows // groups)
    flat = node_groups.reshape(-1)
    onehot = (flat[:, None] == jnp.arange(groups, dtype=jnp.int32)[None, :]).astype(jnp.int32)
    rank = jnp.sum((jnp.cumsum(onehot, axis=0) - onehot) * onehot, axis=1)
    target = flat * slots + rank
    place = (target[None, :] == jnp.arange(groups * slots, dtype=jnp.int32)[:, None]).astype(
        jnp.float32
    )
    spread = jnp.sum(place.reshape(groups * slots, tok_rows, picks), axis=2).astype(jnp.bfloat16)
    scores = jax.nn.sigmoid(gate_logits)
    total = jnp.sum(scores, axis=1, keepdims=True)
    weights = route_scale * scores / total
    slot_weight = jnp.dot(place, weights.reshape(-1, 1), precision=lax.Precision.HIGHEST)[:, 0]
    send_w = slot_weight.astype(jnp.bfloat16).reshape(groups, slots)
    send_x = (
        jnp.dot(spread, tokens, preferred_element_type=jnp.float32)
        .astype(jnp.bfloat16)
        .reshape(groups, slots, feat)
    )
    send_c = (
        jnp.dot(spread, cotangent, preferred_element_type=jnp.float32)
        .astype(jnp.bfloat16)
        .reshape(groups, slots, feat)
    )
    up_local = up_weight[0]
    down_local = down_weight[0]
    rows_x = lax.all_to_all(send_x, "wide", split_axis=0, concat_axis=0, tiled=True)
    rows_c = lax.all_to_all(send_c, "wide", split_axis=0, concat_axis=0, tiled=True)
    rows_w = lax.all_to_all(send_w, "wide", split_axis=0, concat_axis=0, tiled=True)
    sources, count = rows_w.shape
    flat_x = rows_x.reshape(sources * count, feat)
    flat_c = rows_c.reshape(sources * count, feat)
    flat_w = rows_w.reshape(sources * count, 1).astype(jnp.float32)
    up_part = jnp.dot(flat_x, up_local, preferred_element_type=jnp.float32)
    back_part = lax.dot_general(
        flat_c, down_local, (((1,), (1,)), ((), ())), preferred_element_type=jnp.float32
    )
    pre = lax.psum(up_part.astype(jnp.bfloat16), "narrow").astype(jnp.float32)
    grad = lax.psum(back_part.astype(jnp.bfloat16), "narrow").astype(jnp.float32)
    hidden = jax.nn.silu(pre).astype(jnp.bfloat16)
    score = jnp.sum(hidden.astype(jnp.float32) * grad, axis=1)
    hidden_grad = (flat_w * grad * silu_slope(pre)).astype(jnp.bfloat16)
    output = (flat_w * jnp.dot(hidden, down_local, preferred_element_type=jnp.float32)).astype(
        jnp.bfloat16
    )
    input_grad = lax.dot_general(
        hidden_grad, up_local, (((1,), (1,)), ((), ())), preferred_element_type=jnp.float32
    ).astype(jnp.bfloat16)
    score_rows = score.astype(jnp.bfloat16).reshape(sources, count)
    back_y = lax.all_to_all(
        output.reshape(sources, count, feat), "wide", split_axis=0, concat_axis=0, tiled=True
    )
    back_g = lax.all_to_all(
        input_grad.reshape(sources, count, feat), "wide", split_axis=0, concat_axis=0, tiled=True
    )
    back_q = lax.all_to_all(score_rows, "wide", split_axis=0, concat_axis=0, tiled=True)
    rows_y = back_y.reshape(groups * slots, feat)
    rows_g = back_g.reshape(groups * slots, feat)
    contract = (((0,), (0,)), ((), ()))
    mixed = lax.dot_general(spread, rows_y, contract, preferred_element_type=jnp.float32).astype(
        jnp.bfloat16
    )
    grad_sum = lax.dot_general(spread, rows_g, contract, preferred_element_type=jnp.float32)
    samples = advantages.shape[0]
    match = sample_ids[:, None] == jnp.arange(samples, dtype=jnp.int32)[None, :]
    advantage = jnp.sum(jnp.where(match, advantages[None, :], 0.0), axis=1)
    token_grad = (advantage[:, None] * grad_sum).astype(jnp.bfloat16)
    picked = lax.dot_general(
        place, back_q.reshape(-1, 1).astype(jnp.float32), contract, precision=lax.Precision.HIGHEST
    )
    picked = picked.reshape(tok_rows, picks)
    mean_score = jnp.sum(weights * picked, axis=1, keepdims=True) / route_scale
    logit_grad = (
        advantage[:, None] * (route_scale / total) * (picked - mean_score) * scores * (1.0 - scores)
    )
    return (mixed, token_grad, logit_grad)


def solution(mesh):
    in_specs = (
        P("wide", "narrow"),
        P("wide", "narrow"),
        P("wide", None),
        P("wide", None),
        P("wide"),
        P(),
        P("wide", "narrow", None),
        P("wide", None, "narrow"),
    )
    out_specs = (P("wide", "narrow"), P("wide", "narrow"), P("wide", None))
    return jax.shard_map(shards, mesh=mesh, in_specs=in_specs, out_specs=out_specs, check_vma=False)
```

profile of v0, /device:TPU:1, one launch (start us, length us, event | category | flops | bytes accessed | tf_op | source)
XLA Modules:
  0.0 251.2 jit_solution(13840550750356337356)
XLA Ops:
  7.2 0.0 copy-start
  7.2 0.9 copy.41
  8.0 0.1 eq.82
  8.1 0.1 fusion.24
  8.2 0.2 reduce_window_sum.11
  8.4 0.2 select_reduce_fusion
  8.6 0.0 copy-start.4
  8.6 0.1 reduce_sum.57
  8.7 0.0 copy-start.7
  8.7 0.1 copy.42
  8.8 0.6 copy-done.7
  9.4 0.1 convert_reduce_fusion
  9.5 0.0 copy-done.4
  9.5 0.2 convolution_convert_fusion.2
  9.7 0.8 reshape.155
  10.6 25.4 %all-to-all-start.3 = ((bf16[128,2,512]{2,1,0:T(2,128)(2,1)}), bf16[128,2,512]{2,1,0:T(2,128)(2,1)S(1)}, u32[]{:S(2)}, u32[]{:S(2)}) async-start(bf16[128,2,512]{2,1,0:T(2,128)(2,1)} %reshape.155), calls=%async_computation.3 | async-start | bytes 524288 | tf_op jit(solution)/shard_map/all_to_all | solution.py:47
  35.9 0.0 copy-done.5
  35.9 0.0 copy-start.1
  35.9 0.2 convolution_convert_fusion.3
  36.2 0.8 reshape.151
  37.0 13.2 %all-to-all-done.3 = bf16[128,2,512]{2,1,0:T(2,128)(2,1)S(1)} async-done(((bf16[128,2,512]{2,1,0:T(2,128)(2,1)}), bf16[128,2,512]{2,1,0:T(2,128)(2,1)S(1)}, u32[]{:S(2)}, u32[]{:S(2)}) %all-to-all-start.3) | async-done | bytes 262176 | tf_op jit(solution)/shard_map/all_to_all | solution.py:47
  50.2 7.0 %all-to-all-start.1 = ((bf16[128,2,512]{2,1,0:T(2,128)(2,1)}), bf16[128,2,512]{2,1,0:T(2,128)(2,1)S(1)}, u32[]{:S(2)}, u32[]{:S(2)}) async-start(bf16[128,2,512]{2,1,0:T(2,128)(2,1)} %reshape.151), calls=%async_computation.1 | async-start | bytes 524288 | tf_op jit(solution)/shard_map/all_to_all | solution.py:46
  57.1 0.0 all-reduce.3.cloned.1.call-start
  57.2 0.1 reshape.156
  57.3 0.0 copy-done.1
  57.3 1.3 convolution_convert_fusion
  58.6 12.9 %all-to-all-done.1 = bf16[128,2,512]{2,1,0:T(2,128)(2,1)S(1)} async-done(((bf16[128,2,512]{2,1,0:T(2,128)(2,1)}), bf16[128,2,512]{2,1,0:T(2,128)(2,1)S(1)}, u32[]{:S(2)}, u32[]{:S(2)}) %all-to-all-start.1) | async-done | bytes 262176 | tf_op jit(solution)/shard_map/all_to_all | solution.py:46
  71.5 0.1 reshape.152
  71.6 0.0 copy-done
  71.6 1.3 convolution_convert_fusion.1
  72.8 0.0 all-reduce.3.cloned.1.call-update
  72.9 0.2 broadcast_compare_fusion
  73.1 75.7 %all-reduce.3.cloned.1.call-done = (bf16[256,1024]{1,0:T(8,128)(2,1)}, bf16[256,1024]{1,0:T(8,128)(2,1)}) async-done(((bf16[256,1024]{1,0:T(8,128)(2,1)}, bf16[256,1024]{1,0:T(8,128)(2,1)}), (bf16[256,1024]{1,0:T(8,128)(2,1)}, bf16[256,1024]{1,0:T(8,128)(2,1)})) %all-reduce.3.cloned.1.call-update) | async-done | bytes 1048592 | tf_op jit(solution)/shard_map/psum | solution.py:57
  148.8 1.7 fusion.4
  150.5 0.8 convert_element_type.106
  151.3 19.3 %all-to-all-start.5 = ((bf16[128,1,2]{2,1,0:T(2,128)(2,1)}), bf16[128,1,2]{2,1,0:T(2,128)(2,1)S(1)}, u32[]{:S(2)}, u32[]{:S(2)}) async-start(bf16[128,1,2]{2,1,0:T(2,128)(2,1)} %convert_element_type.106), calls=%async_computation.5 | async-start | bytes 131072 | tf_op jit(solution)/shard_map/all_to_all | solution.py:75
  170.6 0.0 copy-done.6
  170.6 11.5 %all-to-all-done.5 = bf16[128,1,2]{2,1,0:T(2,128)(2,1)S(1)} async-done(((bf16[128,1,2]{2,1,0:T(2,128)(2,1)}), bf16[128,1,2]{2,1,0:T(2,128)(2,1)S(1)}, u32[]{:S(2)}, u32[]{:S(2)}) %all-to-all-start.5) | async-done | bytes 544 | tf_op jit(solution)/shard_map/all_to_all | solution.py:75
  182.1 0.2 reduce.1
  182.3 0.1 reshape.163
  182.5 0.2 fusion.21
  182.7 0.1 copy.43
  182.8 0.1 reshape.161
  183.0 0.1 fusion.19
  183.1 0.2 copy.44
  183.3 16.7 %all_to_all.32 = bf16[128,1,2]{2,1,0:T(2,128)(2,1)S(1)} all-to-all(bf16[128,1,2]{2,1,0:T(2,128)(2,1)S(1)} %copy.44), channel_id=1, replica_groups=mesh['wide'=128,'narrow'=8] {'wide'}, dimensions={0} | all-to-all | bytes 1024 | tf_op jit(solution)/shard_map/all_to_all | solution.py:48
  200.0 0.2 convert_reduce_fusion.1
  200.2 0.1 reshape.160
  200.4 0.0 copy-done.3
  200.4 0.0 copy-done.2
  200.4 0.7 convolution_convert_fusion.4
  201.1 0.8 reshape.157
  201.9 6.0 %all-to-all-start.4 = ((bf16[128,2,512]{2,1,0:T(2,128)(2,1)}), bf16[128,2,512]{2,1,0:T(2,128)(2,1)S(1)}, u32[]{:S(2)}, u32[]{:S(2)}) async-start(bf16[128,2,512]{2,1,0:T(2,128)(2,1)} %reshape.157), calls=%async_computation.4 | async-start | bytes 524288 | tf_op jit(solution)/shard_map/all_to_all | solution.py:72
  207.9 0.2 select_reduce_fusion.1
  208.1 0.5 fusion
  208.6 0.8 reshape.153
  209.4 12.9 %all-to-all-done.4 = bf16[128,2,512]{2,1,0:T(2,128)(2,1)S(1)} async-done(((bf16[128,2,512]{2,1,0:T(2,128)(2,1)}), bf16[128,2,512]{2,1,0:T(2,128)(2,1)S(1)}, u32[]{:S(2)}, u32[]{:S(2)}) %all-to-all-start.4) | async-done | bytes 262176 | tf_op jit(solution)/shard_map/all_to_all | solution.py:72
  222.2 6.9 %all-to-all-start.2 = ((bf16[128,2,512]{2,1,0:T(2,128)(2,1)}), bf16[128,2,512]{2,1,0:T(2,128)(2,1)S(1)}, u32[]{:S(2)}, u32[]{:S(2)}) async-start(bf16[128,2,512]{2,1,0:T(2,128)(2,1)} %reshape.153), calls=%async_computation.2 | async-start | bytes 524288 | tf_op jit(solution)/shard_map/all_to_all | solution.py:69
  229.2 0.6 subtract_multiply_fusion
  229.8 0.1 reshape.158
  229.9 0.8 fusion.1
  230.6 12.9 %all-to-all-done.2 = bf16[128,2,512]{2,1,0:T(2,128)(2,1)S(1)} async-done(((bf16[128,2,512]{2,1,0:T(2,128)(2,1)}), bf16[128,2,512]{2,1,0:T(2,128)(2,1)S(1)}, u32[]{:S(2)}, u32[]{:S(2)}) %all-to-all-start.2) | async-done | bytes 262176 | tf_op jit(solution)/shard_map/all_to_all | solution.py:69
  243.5 0.1 reshape.154
  243.6 0.8 convolution_convert_fusion.5
  (15 shorter events, 0.1 us)
Async XLA Ops:
  7.2 64.4 %copy-start = (bf16[1,512,1024]{2,1,0:T(8,128)(2,1)S(1)}, bf16[1,512,1024]{2,1,0:T(8,128)(2,1)}, u32[]{:S(2)}) copy-start(bf16[1,512,1024]{2,1,0:T(8,128)(2,1)} %param.14) | copy-start | bytes 3145732
  8.6 0.9 copy-start.4
  8.7 0.7 copy-start.7
  10.5 25.4 %copy-start.5 = (bf16[32,512]{1,0:T(8,128)(2,1)S(1)}, bf16[32,512]{1,0:T(8,128)(2,1)}, u32[]{:S(2)}) copy-start(bf16[32,512]{1,0:T(8,128)(2,1)} %param.8) | copy-start | bytes 98308
  10.6 39.6 %all-to-all-start.3 = ((bf16[128,2,512]{2,1,0:T(2,128)(2,1)}), bf16[128,2,512]{2,1,0:T(2,128)(2,1)S(1)}, u32[]{:S(2)}, u32[]{:S(2)}) async-start(bf16[128,2,512]{2,1,0:T(2,128)(2,1)} %reshape.155), calls=%async_computation.3 | async-start | bytes 524288 | tf_op jit(solution)/shard_map/all_to_all | solution.py:47
  35.9 21.3 %copy-start.1 = (bf16[1,1024,512]{2,1,0:T(8,128)(2,1)S(1)}, bf16[1,1024,512]{2,1,0:T(8,128)(2,1)}, u32[]{:S(2)}) copy-start(bf16[1,1024,512]{2,1,0:T(8,128)(2,1)} %param.15) | copy-start | bytes 3145732
  50.2 21.3 %all-to-all-start.1 = ((bf16[128,2,512]{2,1,0:T(2,128)(2,1)}), bf16[128,2,512]{2,1,0:T(2,128)(2,1)S(1)}, u32[]{:S(2)}, u32[]{:S(2)}) async-start(bf16[128,2,512]{2,1,0:T(2,128)(2,1)} %reshape.151), calls=%async_computation.1 | async-start | bytes 524288 | tf_op jit(solution)/shard_map/all_to_all | solution.py:46
  57.1 91.7 %all-reduce.3.cloned.1.call-start = ((), (), s32[]{:S(2)}) async-start(), calls=%async_computation.6 | async-start | bytes 2097152 | tf_op jit(solution)/shard_map/psum | solution.py:57
  148.8 21.8 %copy-start.6 = (f32[32,4]{0,1:T(4,128)S(1)}, f32[32,4]{0,1:T(4,128)}, u32[]{:S(2)}) copy-start(f32[32,4]{0,1:T(4,128)} %param.10) | copy-start | bytes 1540
  148.8 51.5 %copy-start.3 = (bf16[256,1024]{1,0:T(8,128)(2,1)S(1)}, bf16[256,1024]{1,0:T(8,128)(2,1)}, u32[]{:S(2)}) copy-start(bf16[256,1024]{1,0:T(8,128)(2,1)} %get-tuple-element.4) | copy-start | bytes 1572868
  150.5 49.9 %copy-start.2 = (bf16[256,1024]{1,0:T(8,128)(2,1)S(1)}, bf16[256,1024]{1,0:T(8,128)(2,1)}, u32[]{:S(2)}) copy-start(bf16[256,1024]{1,0:T(8,128)(2,1)} %get-tuple-element.3) | copy-start | bytes 1572868
  151.3 30.9 %all-to-all-start.5 = ((bf16[128,1,2]{2,1,0:T(2,128)(2,1)}), bf16[128,1,2]{2,1,0:T(2,128)(2,1)S(1)}, u32[]{:S(2)}, u32[]{:S(2)}) async-start(bf16[128,1,2]{2,1,0:T(2,128)(2,1)} %convert_element_type.106), calls=%async_computation.5 | async-start | bytes 131072 | tf_op jit(solution)/shard_map/all_to_all | solution.py:75
  201.9 6.0 %copy-start.8 = (f32[64]{0:T(128)S(1)}, f32[64]{0:T(128)}, u32[]{:S(2)}) copy-start(f32[64]{0:T(128)} %param.13) | copy-start | bytes 772
  201.9 6.0 %copy-start.9 = (s32[32]{0:T(128)S(1)}, s32[32]{0:T(128)}, u32[]{:S(2)}) copy-start(s32[32]{0:T(128)} %param.12) | copy-start | bytes 388
  201.9 20.3 %all-to-all-start.4 = ((bf16[128,2,512]{2,1,0:T(2,128)(2,1)}), bf16[128,2,512]{2,1,0:T(2,128)(2,1)S(1)}, u32[]{:S(2)}, u32[]{:S(2)}) async-start(bf16[128,2,512]{2,1,0:T(2,128)(2,1)} %reshape.157), calls=%async_computation.4 | async-start | bytes 524288 | tf_op jit(solution)/shard_map/all_to_all | solution.py:72
  222.2 21.3 %all-to-all-start.2 = ((bf16[128,2,512]{2,1,0:T(2,128)(2,1)}), bf16[128,2,512]{2,1,0:T(2,128)(2,1)S(1)}, u32[]{:S(2)}, u32[]{:S(2)}) async-start(bf16[128,2,512]{2,1,0:T(2,128)(2,1)} %reshape.153), calls=%async_computation.2 | async-start | bytes 524288 | tf_op jit(solution)/shard_map/all_to_all | solution.py:69
Sparse Core Ops, SparseCore 0:
  73.0 75.8 all-reduce.2
where the time goes:
time: 252 us; the launch traced here: 251 us
  waiting for transfers between devices  139 us (55%)
  starting transfers between devices  64.6 us (26%)
  blocking collectives  16.7 us (7%)
  between operations  14.3 us (6%)
  local copies, waits for them, and re-layouts  6.86 us (3%)
  matrix products  6.07 us (2%)
  other arithmetic  3.61 us (1%)
    psum x1, waiting for transfers between devices, shards(): pre = lax.psum(up_part.astype(jnp.bfloat16), 'narrow').astype(jnp.float32)  75.7 us
    all_to_all x1, starting transfers between devices, shards(): lax.all_to_all(send_c, 'wide', split_axis=0, concat_axis=0, tiled=True)  25.4 us
    all_to_all x1, starting transfers between devices, shards(): lax.all_to_all(score_rows, 'wide', split_axis=0, concat_axis=0, tiled=True)  19.3 us
    all_to_all x1, blocking collectives, shards(): lax.all_to_all(send_w, 'wide', split_axis=0, concat_axis=0, tiled=True)  16.7 us
    all_to_all x1, waiting for transfers between devices, shards(): lax.all_to_all(send_c, 'wide', split_axis=0, concat_axis=0, tiled=True)  13.2 us
    all_to_all x1, waiting for transfers between devices, shards(): lax.all_to_all(send_x, 'wide', split_axis=0, concat_axis=0, tiled=True)  12.9 us
    all_to_all x1, waiting for transfers between devices, shards(): lax.all_to_all(input_grad.reshape(sources, count, feat), 'wide', split_ax...  12.9 us
    all_to_all x1, waiting for transfers between devices, shards(): lax.all_to_all(output.reshape(sources, count, feat), 'wide', split_axis=0...  12.9 us
  transfers between devices with their start and end apart: 6, of which 6 were waited for; matrix products, arithmetic and copies ran while one was open for 2% of the time, Pallas kernels for 0%

commit v1 on v0

v1 whole, which is shorter than its diff:
```python
import functools
import math

import jax
import jax.numpy as jnp
from jax import lax
from jax.experimental import pallas as pl
from jax.experimental.pallas import tpu as pltpu
from jax.sharding import PartitionSpec as P

MESH = pl.DeviceIdType.MESH
f32, bf16 = jnp.float32, jnp.bfloat16
SCALE = 2.5
CORES = 2
SLOTS = 2


def dot(a, b):
    return lax.dot_general(a, b, (((1,), (0,)), ((), ())), preferred_element_type=f32)


def dot_nt(a, b):
    return lax.dot_general(a, b, (((1,), (1,)), ((), ())), preferred_element_type=f32)


def dot_tn(a, b):
    return lax.dot_general(a, b, (((0,), (0,)), ((), ())), preferred_element_type=f32)


def rows_at(index, size):
    return pl.ds(pl.multiple_of(index * size, size), size)


def kernel(
    side, ring,
    tok_ref, cot_ref, gate_ref, group_ref, id_ref, adv_ref, up_hbm, down_hbm,
    mixed_ref, tgrad_ref, lgrad_ref,
    up_ref, down_ref, send, mid, mid2, land, part, inbox, both, outrow, score_box,
    w_sem, st_send, st_recv, ring_send, ring_recv, ag_send, ag_recv, tail_send, tail_recv,
):
    wide, me = lax.axis_index("wide"), lax.axis_index("narrow")
    my_y = lax.div(wide, side * CORES)
    my_z = lax.rem(lax.div(wide, CORES), side)
    my_c = lax.rem(wide, CORES)
    toks, feat = tok_ref.shape
    rows = send.shape[1]
    ff = up_ref.shape[1]
    big, small = rows // side, rows // (side * CORES)
    chunk = rows // ring
    half = ring // 2
    right, left = lax.rem(me + 1, ring), lax.rem(me + ring - 1, ring)

    def wide_of(y, z, c):
        return (y * side + z) * CORES + c

    def near(stream, k):
        if stream == 0:
            spot = lax.rem(my_z + k, side)
            return spot, wide_of(my_y, spot, my_c)
        spot = lax.rem(my_y + k, side)
        return spot, wide_of(spot, my_z, my_c)

    def far(stream, k):
        if stream == 0:
            spot = lax.rem(my_y * CORES + my_c + k, side * CORES)
            return spot, wide_of(lax.div(spot, CORES), my_z, lax.rem(spot, CORES))
        spot = lax.rem(my_z * CORES + my_c + k, side * CORES)
        return spot, wide_of(my_y, lax.div(spot, CORES), lax.rem(spot, CORES))

    my_near = (my_z, my_y)
    my_far = (my_y * CORES + my_c, my_z * CORES + my_c)

    barrier = pltpu.get_barrier_semaphore()

    def greet(target, narrow):
        pl.semaphore_signal(barrier, inc=1, device_id=(target, narrow), device_id_type=MESH)

    @pl.loop(1, side * CORES)
    def _(k):
        greet(far(1, k)[1], me)

    @pl.loop(1, side)
    def _(k):
        spot = lax.rem(my_y + k, side)
        greet(wide_of(spot, my_z, 0), me)
        greet(wide_of(spot, my_z, 1), me)

    @pl.loop(1, ring)
    def _(k):
        greet(wide, lax.rem(me + k, ring))

    greeted = side * CORES - 1 + (side - 1) * CORES + ring - 1

    up_copy = pltpu.make_async_copy(up_hbm.at[0], up_ref, w_sem.at[0])
    down_copy = pltpu.make_async_copy(down_hbm.at[0], down_ref, w_sem.at[1])
    up_copy.start()
    down_copy.start()

    groups = group_ref[...]
    gate = gate_ref[...]
    picks = groups.shape[1]
    scores = 1.0 / (1.0 + jnp.exp(-gate))
    total = jnp.sum(scores, axis=1, keepdims=True)
    weights = SCALE * scores / total
    lane = lax.broadcasted_iota(jnp.int32, (toks, rows), 1)
    pair = lane >> 1
    core, spot = pair & 1, pair >> 1
    slot = (lane & 1).astype(f32)
    first, second = spot // side, spot % side
    group_of = (wide_of(second, first, core), pair)
    earlier = (
        lax.broadcasted_iota(jnp.int32, (toks, toks), 1)
        < lax.broadcasted_iota(jnp.int32, (toks, toks), 0)
    ).astype(bf16)

    def route(stream):
        named = [groups[:, j : j + 1] == group_of[stream] for j in range(picks)]
        hit = functools.reduce(jnp.logical_or, named).astype(f32)
        rank = dot(earlier, hit.astype(bf16))
        mine = jnp.where(rank == slot, hit, 0.0)
        weighted = sum(jnp.where(named[j], weights[:, j : j + 1], 0.0) for j in range(picks))
        return mine, (mine * weighted).astype(bf16), named

    sources = (tok_ref, cot_ref)
    routes = [route(stream) for stream in range(2)]
    for stream in range(2):
        send[stream] = dot_tn(routes[stream][0].astype(bf16), sources[stream][...]).astype(bf16)

    def swap(forward):
        i = lax.broadcasted_iota(jnp.int32, (rows, rows), 0)
        j = lax.broadcasted_iota(jnp.int32, (rows, rows), 1)
        out, source = (i, j) if forward else (j, i)
        s, b, c, a = out & 1, (out >> 1) % side, (out >> 1) // side % CORES, (out >> 1) // (side * CORES)
        return (source == ((b * side + a) * CORES + c) * SLOTS + s).astype(bf16)

    def cross():
        i = lax.broadcasted_iota(jnp.int32, (rows, rows), 0)
        j = lax.broadcasted_iota(jnp.int32, (rows, rows), 1)
        s, b, c, a = i & 1, (i >> 1) % side, (i >> 1) // side % CORES, (i >> 1) // (side * CORES)
        return (j == ((b * CORES + c) * side + a) * SLOTS + s).astype(bf16)

    def remote(src, dst, s_sem, r_sem, target, narrow):
        return pltpu.make_async_remote_copy(
            src_ref=src, dst_ref=dst, send_sem=s_sem, recv_sem=r_sem,
            device_id=(target, narrow), device_id_type=MESH,
        )

    def near_stage(stage, stream, src, dst):
        mine = my_near[stream]

        @pl.loop(1, side)
        def _(k):
            spot, target = near(stream, k)
            remote(
                src.at[stream, rows_at(spot, big)], dst.at[stream, rows_at(mine, big)],
                st_send.at[stage, stream], st_recv.at[stage, stream], target, me,
            ).start()

        dst[stream, rows_at(mine, big)] = src[stream, rows_at(mine, big)]

    def far_stage(stage, stream, src, dst):
        mine = my_far[stream]

        @pl.loop(1, side * CORES)
        def _(k):
            spot, target = far(stream, k)
            remote(
                src.at[stream, rows_at(spot, small)], dst.at[stream, rows_at(mine, small)],
                st_send.at[stage, stream], st_recv.at[stage, stream], target, me,
            ).start()

        dst[stream, rows_at(mine, small)] = src[stream, rows_at(mine, small)]

    def landed(stage, stream, dst, part_of):
        view = dst.at[stream, pl.ds(0, rows - part_of)]
        pltpu.make_async_copy(view, view, st_recv.at[stage, stream]).wait()

    def gone(stage, stream, src, part_of):
        view = src.at[stream, pl.ds(0, rows - part_of)]
        pltpu.make_async_copy(view, view, st_send.at[stage, stream]).wait()

    pl.semaphore_wait(barrier, greeted)

    for stream in range(2):
        near_stage(0, stream, send, mid.at[0])
    for stream in range(2):
        landed(0, stream, mid.at[0], big)
        mid2[0, stream] = dot(swap(True), mid[0, stream]).astype(bf16)
        far_stage(1, stream, mid2.at[0], land)

    def ring_copy(kind, way, distance):
        owner = lax.rem(me + (distance if way == 0 else ring - distance), ring)
        return remote(
            part.at[kind, rows_at(owner, chunk)], inbox.at[kind, way, distance - 1],
            ring_send.at[kind, way, distance - 1], ring_recv.at[kind, way, distance - 1],
            wide, right if way == 0 else left,
        )

    def add_arrived(kind, way, distance):
        ring_copy(kind, way, distance).wait_recv()
        owner = lax.rem(me + (distance - 1 if way == 0 else ring - distance + 1), ring)
        spot = rows_at(owner, chunk)
        part[kind, spot] = (
            part[kind, spot].astype(f32) + inbox[kind, way, distance - 1].astype(f32)
        ).astype(bf16)

    def longest(kind, way):
        return half if kind == way else half - 1

    tile = min(256, ff)
    up_copy.wait()
    landed(1, 0, land, small)
    rows_x = land[0]

    @pl.loop(0, ff // tile)
    def _(n):
        cols = pl.ds(pl.multiple_of(n * tile, tile), tile)
        part[0, :, cols] = dot(rows_x, up_ref[:, cols]).astype(bf16)

    for way in (0, 1):
        if longest(0, way) > 0:
            ring_copy(0, way, longest(0, way)).start()
    down_copy.wait()
    landed(1, 1, land, small)
    rows_c = dot(cross(), land[1]).astype(bf16)

    @pl.loop(0, ff // tile)
    def _(n):
        cols = pl.ds(pl.multiple_of(n * tile, tile), tile)
        part[1, :, cols] = dot_nt(rows_c, down_ref[cols, :]).astype(bf16)

    for way in (1, 0):
        if longest(1, way) > 0:
            ring_copy(1, way, longest(1, way)).start()
    for later in range(half - 1):
        for kind, way in ((0, 0), (1, 1), (0, 1), (1, 0)):
            distance = longest(kind, way) - later
            if distance >= 2:
                add_arrived(kind, way, distance)
                ring_copy(kind, way, distance - 1).start()

    own = rows_at(me, chunk)
    sums = []
    for kind in (0, 1):
        acc = part[kind, own].astype(f32)
        for way in (0, 1):
            if longest(kind, way) > 0:
                ring_copy(kind, way, 1).wait_recv()
                acc = acc + inbox[kind, way, 0].astype(f32)
        sums.append(acc)
    pre, grad = sums
    sig = 1.0 / (1.0 + jnp.exp(-pre))
    both[0, own] = (pre * sig).astype(bf16)
    both[1, own] = (grad * (sig * (1.0 + pre * (1.0 - sig)))).astype(bf16)

    def pass_on(kind, way, distance):
        owner = lax.rem(me + (ring - distance + 1 if way == 0 else distance - 1), ring)
        view = both.at[kind, rows_at(owner, chunk)]
        return remote(
            view, view, ag_send.at[kind, way, distance - 1], ag_recv.at[kind, way, distance - 1],
            wide, right if way == 0 else left,
        )

    for kind in (0, 1):
        for way in (0, 1):
            if longest(kind, way) > 0:
                pass_on(kind, way, 1).start()
    for distance in range(1, half + 1):
        for kind, way in ((0, 0), (0, 1), (1, 0), (1, 1)):
            if distance <= longest(kind, way):
                pass_on(kind, way, distance).wait_recv()
                if distance < longest(kind, way):
                    pass_on(kind, way, distance + 1).start()

    wide_tile = min(256, feat)

    @pl.loop(0, feat // wide_tile)
    def _(n):
        cols = pl.ds(pl.multiple_of(n * wide_tile, wide_tile), wide_tile)
        outrow[0, 0, :, cols] = dot(both[0], down_ref[:, cols]).astype(bf16)

    far_stage(2, 0, outrow.at[0], mid.at[1])

    @pl.loop(0, feat // wide_tile)
    def _(n):
        cols = pl.ds(pl.multiple_of(n * wide_tile, wide_tile), wide_tile)
        mixed_rows = dot_nt(both[1], up_ref[cols, :]).astype(bf16)
        outrow[0, 1, :, cols] = dot(cross(), mixed_rows).astype(bf16)

    far_stage(2, 1, outrow.at[0], mid.at[1])
    for stream in range(2):
        landed(2, stream, mid.at[1], small)
        mid2[1, stream] = dot(swap(False), mid[1, stream]).astype(bf16)
        near_stage(3, stream, mid2.at[1], outrow.at[1])

    landed(3, 0, outrow.at[1], big)
    back = outrow[1, 0]
    mine, weighted, named = routes[0]
    products = dot_nt(cot_ref[...], back) * mine
    lane4 = lax.broadcasted_iota(jnp.int32, (toks, 128), 1)
    row4 = lax.broadcasted_iota(jnp.int32, (toks, 128), 0)
    packed = jnp.zeros((toks, 128), f32)
    for j in range(picks):
        column = jnp.sum(jnp.where(named[j], products, 0.0), axis=1, keepdims=True)
        packed = jnp.where(lane4 == row4 * picks + j, column, packed)
    score_box[rows_at(me, 8)] = jnp.broadcast_to(jnp.sum(packed, axis=0, keepdims=True), (8, 128))

    @pl.loop(1, ring)
    def _(k):
        view = score_box.at[rows_at(me, 8)]
        remote(view, view, tail_send, tail_recv, wide, lax.rem(me + k, ring)).start()

    mixed_ref[...] = dot(weighted, back).astype(bf16)
    ids = id_ref[...].astype(f32)
    square = lax.broadcasted_iota(jnp.int32, (toks, toks), 0) == lax.broadcasted_iota(
        jnp.int32, (toks, toks), 1
    )
    id_column = jnp.sum(jnp.where(square, ids, 0.0), axis=1, keepdims=True)
    samples = adv_ref.shape[1]
    match = id_column == lax.broadcasted_iota(jnp.int32, (toks, samples), 1).astype(f32)
    advantage = jnp.sum(jnp.where(match, adv_ref[...], 0.0), axis=1, keepdims=True)
    landed(3, 1, outrow.at[1], big)
    tgrad_ref[...] = (advantage * dot(routes[1][1], outrow[1, 1])).astype(bf16)

    tail_view = score_box.at[pl.ds(0, (ring - 1) * 8)]
    pltpu.make_async_copy(tail_view, tail_view, tail_recv).wait()
    summed = score_box[pl.ds(0, 8)]
    for other in range(1, ring):
        summed = summed + score_box[pl.ds(other * 8, 8)]
    spread = jnp.broadcast_to(summed[0:1], (toks, 128))
    lane_pick = lax.broadcasted_iota(jnp.int32, (toks, picks), 1)
    picked = jnp.zeros((toks, picks), f32)
    for j in range(picks):
        column = jnp.sum(jnp.where(lane4 == row4 * picks + j, spread, 0.0), axis=1, keepdims=True)
        picked = jnp.where(lane_pick == j, column, picked)
    mean_score = jnp.sum(weights * picked, axis=1, keepdims=True) / SCALE
    lgrad_ref[...] = (
        advantage * (SCALE / total) * (picked - mean_score) * scores * (1.0 - scores)
    )

    for stream in range(2):
        gone(0, stream, send, big)
        gone(1, stream, mid2.at[0], small)
        gone(2, stream, outrow.at[0], small)
        gone(3, stream, mid2.at[1], big)
    for kind in (0, 1):
        for way in (0, 1):
            for distance in range(1, longest(kind, way) + 1):
                ring_copy(kind, way, distance).wait_send()
                pass_on(kind, way, distance).wait_send()
    pltpu.make_async_copy(tail_view, tail_view, tail_send).wait()


def solution(mesh):
    ring = mesh.shape["narrow"]
    side = math.isqrt(mesh.shape["wide"] // CORES)

    def step(tokens, cotangent, gate, groups, ids, advantages, up, down):
        toks, feat = tokens.shape
        ff = up.shape[2]
        rows = mesh.shape["wide"] * SLOTS
        half = ring // 2
        vmem = pl.BlockSpec(memory_space=pltpu.VMEM)
        hbm = pl.BlockSpec(memory_space=pl.ANY)
        dma = pltpu.SemaphoreType.DMA
        return pl.pallas_call(
            functools.partial(kernel, side, ring),
            out_shape=(
                jax.ShapeDtypeStruct((toks, feat), bf16),
                jax.ShapeDtypeStruct((toks, feat), bf16),
                jax.ShapeDtypeStruct(gate.shape, f32),
            ),
            in_specs=[vmem] * 6 + [hbm] * 2,
            out_specs=[vmem] * 3,
            scratch_shapes=[
                pltpu.VMEM((feat, ff), bf16),
                pltpu.VMEM((ff, feat), bf16),
                pltpu.VMEM((2, rows, feat), bf16),
                pltpu.VMEM((2, 2, rows, feat), bf16),
                pltpu.VMEM((2, 2, rows, feat), bf16),
                pltpu.VMEM((2, rows, feat), bf16),
                pltpu.VMEM((2, rows, ff), bf16),
                pltpu.VMEM((2, 2, half, rows // ring, ff), bf16),
                pltpu.VMEM((2, rows, ff), bf16),
                pltpu.VMEM((2, 2, rows, feat), bf16),
                pltpu.VMEM((ring * 8, 128), f32),
                dma((2,)),
                dma((4, 2)),
                dma((4, 2)),
                dma((2, 2, half)),
                dma((2, 2, half)),
                dma((2, 2, half)),
                dma((2, 2, half)),
                dma,
                dma,
            ],
            compiler_params=pltpu.CompilerParams(
                collective_id=0, has_side_effects=True, vmem_limit_bytes=40 * 1024 * 1024
            ),
            cost_estimate=pl.CostEstimate(
                flops=8 * rows * feat * ff, bytes_accessed=4 * feat * ff, transcendentals=0
            ),
        )(
            tokens, cotangent, gate, groups, ids.reshape(1, toks), advantages.reshape(1, -1), up, down
        )

    in_specs = (
        P("wide", "narrow"),
        P("wide", "narrow"),
        P("wide", None),
        P("wide", None),
        P("wide"),
        P(),
        P("wide", "narrow", None),
        P("wide", None, "narrow"),
    )
    out_specs = (P("wide", "narrow"), P("wide", "narrow"), P("wide", None))
    return jax.shard_map(step, mesh=mesh, in_specs=in_specs, out_specs=out_specs, check_vma=False)
```

time: 252 us -> 101 us (0.40)
  waiting for transfers between devices: 139 us -> 0 us
  Pallas kernels: 0 us -> 93.8 us
  starting transfers between devices: 64.6 us -> 0 us
  blocking collectives: 16.7 us -> 0 us
  between operations: 14.3 us -> 0.68 us
  matrix products: 6.07 us -> 0 us
  other arithmetic: 3.61 us -> 0 us
    pallas_call x0 -> x1, Pallas kernels: none -> 93.8 us  [step(): pl.pallas_call(functools.partial(kernel, side, ring), out_shape=(jax.Shap...]
    psum x1 -> x0, waiting for transfers between devices: 75.7 us -> none  [shards(): pre = lax.psum(up_part.astype(jnp.bfloat16), 'narrow').astype(jnp.float32)]
    all_to_all x5 -> x0, starting transfers between devices: 64.5 us -> none  [the longest x1 25.4 us: shards(): lax.all_to_all(send_c, 'wide', split_axis=0, concat_axis=0, tiled=True)]
    all_to_all x5 -> x0, waiting for transfers between devices: 63.3 us -> none  [the longest x1 13.2 us: shards(): lax.all_to_all(send_c, 'wide', split_axis=0, concat_axis=0, tiled=True)]
    all_to_all x1 -> x0, blocking collectives: 16.7 us -> none  [shards(): lax.all_to_all(send_w, 'wide', split_axis=0, concat_axis=0, tiled=True)]
    dot_general x10 -> x0, matrix products: 6.07 us -> none  [the longest x1 1.29 us: shards(): lax.dot_general(flat_c, down_local, (((1,), (1,)), ((), ())), preferred_e...]
    unnamed x21 -> x18, local copies, waits for them, and re-layouts: 1.5 us -> 5.98 us
    reshape x9 -> x0, local copies, waits for them, and re-layouts: 3.73 us -> none  [the longest x1 0.81 us: shards(): input_grad.reshape(sources, count, feat)]
  transfers between devices with their start and end apart: 6 -> 0, of which waited for: 6 -> 0; matrix products, arithmetic and copies ran while one was open for 2% -> 0% of each run, Pallas kernels for 0% -> 0%
where the time goes in v1:
time: 101 us
  Pallas kernels  93.8 us (93%)
  local copies, waits for them, and re-layouts  6.63 us (7%)
    pallas_call x1, Pallas kernels, step(): pl.pallas_call(functools.partial(kernel, side, ring), out_shape=(jax.Shap...  93.8 us
    unnamed x18, local copies, waits for them, and re-layouts  5.98 us

profile of v1, /device:TPU:1, one launch (start us, length us, event | category | flops | bytes accessed | tf_op | source)
XLA Modules:
  0.0 101.1 jit_solution(17066570625527142266)
XLA Ops:
  0.6 0.0 copy-start.6
  0.6 0.0 copy-start.2
  0.6 0.7 copy-done.6
  1.3 0.1 copy.11.gate_ref
  1.4 0.0 copy-start.4
  1.4 0.0 copy-start.5
  1.4 0.8 copy.12.group_ref
  2.2 0.0 copy-done.2
  2.2 0.0 copy-done.4
  2.2 0.0 copy-done.5
  2.2 0.0 copy-start
  2.2 1.2 %copy-done = bf16[1,512,1024]{2,1,0:T(8,128)(2,1)S(1)} copy-done((bf16[1,512,1024]{2,1,0:T(8,128)(2,1)S(1)}, bf16[1,512,1024]{2,1,0:T(8,128)(2,1)}, u32[]{:S(2)}) %copy-start) | copy-done | bytes 1048600
  3.4 0.0 copy-start.1
  3.4 1.2 %copy-done.1 = bf16[1,1024,512]{2,1,0:T(8,128)(2,1)S(1)} copy-done((bf16[1,1024,512]{2,1,0:T(8,128)(2,1)S(1)}, bf16[1,1024,512]{2,1,0:T(8,128)(2,1)}, u32[]{:S(2)}) %copy-start.1) | copy-done | bytes 1048600
  4.7 0.0 copy-start.3
  4.7 0.8 copy-done.3
  5.4 93.8 %shard_map.103 = (bf16[32,512]{1,0:T(8,128)(2,1)S(1)}, bf16[32,512]{1,0:T(8,128)(2,1)S(1)}, f32[32,4]{1,0:T(8,128)S(1)}) custom-call(bf16[32,512]{1,0:T(8,128)(2,1)S(1)} %copy-done.2, bf16[32,512]{1,0:T(8,128)(2,1)S(1)} %copy-done.3, f32[32,4]{1,0:T(8,128)S(1)} %copy.11.gate_ref, s32[32,4]{1,0:T(8,128)S(1)} %copy.12.group_ref, s32[1,32]{1,0:T(1,128)S(1)} %bitcast.2, ...), custom_call_target="tpu_custom_call" | custom-call | flops 1073741824 | bytes 2097152 | tf_op jit(solution)/shard_map/pallas_call | solution.py:366
  99.2 0.7 copy.13
  99.9 0.6 copy.16
  100.5 0.6 copy.17
Async XLA Ops:
  0.6 0.7 copy-start.6
  0.6 1.6 %copy-start.2 = (bf16[32,512]{1,0:T(8,128)(2,1)S(1)}, bf16[32,512]{1,0:T(8,128)(2,1)}, u32[]{:S(2)}) copy-start(bf16[32,512]{1,0:T(8,128)(2,1)} %tok_ref.1) | copy-start | bytes 98308
  1.4 0.8 copy-start.4
  1.4 0.8 copy-start.5
  2.2 1.2 %copy-start = (bf16[1,512,1024]{2,1,0:T(8,128)(2,1)S(1)}, bf16[1,512,1024]{2,1,0:T(8,128)(2,1)}, u32[]{:S(2)}) copy-start(bf16[1,512,1024]{2,1,0:T(8,128)(2,1)} %up_hbm.1) | copy-start | bytes 3145732
  3.4 1.2 %copy-start.1 = (bf16[1,1024,512]{2,1,0:T(8,128)(2,1)S(1)}, bf16[1,1024,512]{2,1,0:T(8,128)(2,1)}, u32[]{:S(2)}) copy-start(bf16[1,1024,512]{2,1,0:T(8,128)(2,1)} %down_hbm.1) | copy-start | bytes 3145732
  4.7 0.8 copy-start.3

commit v2 on v1

--- a/solution.py
+++ b/solution.py
@@ -33,9 +33,10 @@
 
 def kernel(
     side, ring,
-    tok_ref, cot_ref, gate_ref, group_ref, id_ref, adv_ref, up_hbm, down_hbm,
+    tok_hbm, cot_hbm, gate_hbm, group_hbm, id_hbm, adv_hbm, up_hbm, down_hbm,
     mixed_ref, tgrad_ref, lgrad_ref,
-    up_ref, down_ref, send, mid, mid2, land, part, inbox, both, outrow, score_box,
+    tok_ref, cot_ref, gate_ref, group_ref, id_ref, adv_ref, up_ref, down_ref,
+    send, mid, mid2, land, part, inbox, both, outrow, score_box,
     w_sem, st_send, st_recv, ring_send, ring_recv, ag_send, ag_recv, tail_send, tail_recv,
 ):
     wide, me = lax.axis_index("wide"), lax.axis_index("narrow")
@@ -70,6 +71,17 @@
     my_near = (my_z, my_y)
     my_far = (my_y * CORES + my_c, my_z * CORES + my_c)
 
+    loads = [
+        pltpu.make_async_copy(source, target, w_sem.at[i])
+        for i, (source, target) in enumerate((
+            (group_hbm, group_ref), (gate_hbm, gate_ref), (tok_hbm, tok_ref), (cot_hbm, cot_ref),
+            (id_hbm, id_ref), (adv_hbm, adv_ref), (up_hbm.at[0], up_ref), (down_hbm.at[0], down_ref),
+        ))
+    ]
+    up_copy, down_copy = loads[6:]
+    for load in loads:
+        load.start()
+
     barrier = pltpu.get_barrier_semaphore()
 
     def greet(target, narrow):
@@ -91,17 +103,22 @@
 
     greeted = side * CORES - 1 + (side - 1) * CORES + ring - 1
 
-    up_copy = pltpu.make_async_copy(up_hbm.at[0], up_ref, w_sem.at[0])
-    down_copy = pltpu.make_async_copy(down_hbm.at[0], down_ref, w_sem.at[1])
-    up_copy.start()
-    down_copy.start()
-
-    groups = group_ref[...]
-    gate = gate_ref[...]
-    picks = groups.shape[1]
-    scores = 1.0 / (1.0 + jnp.exp(-gate))
-    total = jnp.sum(scores, axis=1, keepdims=True)
+    for load in loads[:6]:
+        load.wait()
+
+    picks = group_ref.shape[0]
+    scores = 1.0 / (1.0 + jnp.exp(-gate_ref[...]))
+    total = jnp.sum(scores, axis=0, keepdims=True)
     weights = SCALE * scores / total
+    square = lax.broadcasted_iota(jnp.int32, (toks, toks), 0) == lax.broadcasted_iota(
+        jnp.int32, (toks, toks), 1
+    )
+
+    def column(row):
+        return jnp.sum(jnp.where(square, row, 0.0), axis=1, keepdims=True)
+
+    groups = [column(group_ref[j : j + 1].astype(f32)).astype(jnp.int32) for j in range(picks)]
+    weight = [column(weights[j : j + 1]) for j in range(picks)]
     lane = lax.broadcasted_iota(jnp.int32, (toks, rows), 1)
     pair = lane >> 1
     core, spot = pair & 1, pair >> 1
@@ -114,11 +131,11 @@
     ).astype(bf16)
 
     def route(stream):
-        named = [groups[:, j : j + 1] == group_of[stream] for j in range(picks)]
+        named = [groups[j] == group_of[stream] for j in range(picks)]
         hit = functools.reduce(jnp.logical_or, named).astype(f32)
         rank = dot(earlier, hit.astype(bf16))
         mine = jnp.where(rank == slot, hit, 0.0)
-        weighted = sum(jnp.where(named[j], weights[:, j : j + 1], 0.0) for j in range(picks))
+        weighted = sum(jnp.where(named[j], weight[j], 0.0) for j in range(picks))
         return mine, (mine * weighted).astype(bf16), named
 
     sources = (tok_ref, cot_ref)
@@ -188,24 +205,36 @@
         mid2[0, stream] = dot(swap(True), mid[0, stream]).astype(bf16)
         far_stage(1, stream, mid2.at[0], land)
 
+    def nearer(distance):
+        return half - 2 if distance == half >= 3 else distance - 1
+
+    def longest(kind, way):
+        return half if kind == way else half - 1
+
+    def beside(way, hops):
+        return lax.rem(me + (hops if way == 0 else ring - hops), ring)
+
     def ring_copy(kind, way, distance):
-        owner = lax.rem(me + (distance if way == 0 else ring - distance), ring)
+        owner = beside(way, distance)
         return remote(
             part.at[kind, rows_at(owner, chunk)], inbox.at[kind, way, distance - 1],
             ring_send.at[kind, way, distance - 1], ring_recv.at[kind, way, distance - 1],
-            wide, right if way == 0 else left,
+            wide, beside(way, distance - nearer(distance)),
         )
 
-    def add_arrived(kind, way, distance):
-        ring_copy(kind, way, distance).wait_recv()
-        owner = lax.rem(me + (distance - 1 if way == 0 else ring - distance + 1), ring)
-        spot = rows_at(owner, chunk)
-        part[kind, spot] = (
-            part[kind, spot].astype(f32) + inbox[kind, way, distance - 1].astype(f32)
-        ).astype(bf16)
-
-    def longest(kind, way):
-        return half if kind == way else half - 1
+    def add_arrived(kind, way, place):
+        spot = rows_at(beside(way, place), chunk)
+        acc = part[kind, spot].astype(f32)
+        for distance in range(1, longest(kind, way) + 1):
+            if nearer(distance) == place:
+                ring_copy(kind, way, distance).wait_recv()
+                acc = acc + inbox[kind, way, distance - 1].astype(f32)
+        part[kind, spot] = acc.astype(bf16)
+
+    def set_off(kind, way):
+        for distance in range(longest(kind, way), 0, -1):
+            if not any(nearer(d) == distance for d in range(1, longest(kind, way) + 1)):
+                ring_copy(kind, way, distance).start()
 
     tile = min(256, ff)
     up_copy.wait()
@@ -217,9 +246,8 @@
         cols = pl.ds(pl.multiple_of(n * tile, tile), tile)
         part[0, :, cols] = dot(rows_x, up_ref[:, cols]).astype(bf16)
 
-    for way in (0, 1):
-        if longest(0, way) > 0:
-            ring_copy(0, way, longest(0, way)).start()
+    set_off(0, 0)
+    set_off(0, 1)
     down_copy.wait()
     landed(1, 1, land, small)
     rows_c = dot(cross(), land[1]).astype(bf16)
@@ -229,65 +257,99 @@
         cols = pl.ds(pl.multiple_of(n * tile, tile), tile)
         part[1, :, cols] = dot_nt(rows_c, down_ref[cols, :]).astype(bf16)
 
-    for way in (1, 0):
-        if longest(1, way) > 0:
-            ring_copy(1, way, longest(1, way)).start()
-    for later in range(half - 1):
-        for kind, way in ((0, 0), (1, 1), (0, 1), (1, 0)):
-            distance = longest(kind, way) - later
-            if distance >= 2:
-                add_arrived(kind, way, distance)
-                ring_copy(kind, way, distance - 1).start()
+    set_off(1, 1)
+    set_off(1, 0)
+    for place in range(half - 1, 0, -1):
+        for kind, way in ((0, 0), (0, 1), (1, 1), (1, 0)):
+            if any(nearer(d) == place for d in range(1, longest(kind, way) + 1)):
+                add_arrived(kind, way, place)
+                ring_copy(kind, way, place).start()
 
     own = rows_at(me, chunk)
-    sums = []
-    for kind in (0, 1):
+
+    def summed_here(kind):
         acc = part[kind, own].astype(f32)
         for way in (0, 1):
-            if longest(kind, way) > 0:
-                ring_copy(kind, way, 1).wait_recv()
-                acc = acc + inbox[kind, way, 0].astype(f32)
-        sums.append(acc)
-    pre, grad = sums
+            for distance in range(1, longest(kind, way) + 1):
+                if nearer(distance) == 0:
+                    ring_copy(kind, way, distance).wait_recv()
+                    acc = acc + inbox[kind, way, distance - 1].astype(f32)
+        return acc
+
+    def pass_on(kind, way, distance):
+        held = nearer(distance)
+        view = both.at[kind, rows_at(beside(1 - way, held), chunk)]
+        return remote(
+            view, view, ag_send.at[kind, way, distance - 1], ag_recv.at[kind, way, distance - 1],
+            wide, beside(way, distance - held),
+        )
+
+    def hand_on(kind, way, held):
+        for distance in range(1, longest(kind, way) + 1):
+            if nearer(distance) == held:
+                pass_on(kind, way, distance).start()
+
+    def product(kind, owners):
+        spots = [rows_at(owner, chunk) for owner in owners]
+        block = jnp.concatenate([both[kind, spot] for spot in spots], axis=0)
+        out = dot(block, down_ref[...]) if kind == 0 else dot_nt(block, up_ref[...])
+        out = out.astype(bf16)
+        for i, (owner, spot) in enumerate(zip(owners, spots)):
+            outrow[0, kind, spot] = out[i * chunk : (i + 1) * chunk]
+            if kind == 0:
+                for core_to in range(CORES):
+                    goal = owner * CORES + core_to
+                    at_home = goal == my_far[0]
+
+                    @pl.when(at_home)
+                    def _():
+                        mid[1, 0, rows_at(goal, small)] = out[
+                            i * chunk + core_to * small : i * chunk + (core_to + 1) * small
+                        ]
+
+                    @pl.when(jnp.logical_not(at_home))
+                    def _():
+                        remote(
+                            outrow.at[0, 0, rows_at(goal, small)],
+                            mid.at[1, 0, rows_at(my_far[0], small)],
+                            st_send.at[2, 0], st_recv.at[2, 0], wide_of(owner, my_z, core_to), me,
+                        ).start()
+
+    pre = summed_here(0)
     sig = 1.0 / (1.0 + jnp.exp(-pre))
     both[0, own] = (pre * sig).astype(bf16)
-    both[1, own] = (grad * (sig * (1.0 + pre * (1.0 - sig)))).astype(bf16)
-
-    def pass_on(kind, way, distance):
-        owner = lax.rem(me + (ring - distance + 1 if way == 0 else distance - 1), ring)
-        view = both.at[kind, rows_at(owner, chunk)]
-        return remote(
-            view, view, ag_send.at[kind, way, distance - 1], ag_recv.at[kind, way, distance - 1],
-            wide, right if way == 0 else left,
-        )
-
+    for way in (0, 1):
+        hand_on(0, way, 0)
+    slope = sig * (1.0 + pre * (1.0 - sig))
+    both[1, own] = (summed_here(1) * slope).astype(bf16)
+    for way in (1, 0):
+        hand_on(1, way, 0)
     for kind in (0, 1):
-        for way in (0, 1):
-            if longest(kind, way) > 0:
-                pass_on(kind, way, 1).start()
-    for distance in range(1, half + 1):
-        for kind, way in ((0, 0), (0, 1), (1, 0), (1, 1)):
-            if distance <= longest(kind, way):
-                pass_on(kind, way, distance).wait_recv()
-                if distance < longest(kind, way):
-                    pass_on(kind, way, distance + 1).start()
+        product(kind, [me])
+    steps = sorted({nearer(d) for d in range(1, half + 1)})
+    for held in steps:
+        for kind in (0, 1):
+            for way in (0, 1):
+                for distance in range(1, longest(kind, way) + 1):
+                    if nearer(distance) == held:
+                        pass_on(kind, way, distance).wait_recv()
+                        hand_on(kind, way, distance)
+        for kind in (0, 1):
+            product(kind, [
+                beside(1 - way, distance)
+                for way in (0, 1)
+                for distance in range(1, longest(kind, way) + 1)
+                if nearer(distance) == held
+            ])
 
     wide_tile = min(256, feat)
 
     @pl.loop(0, feat // wide_tile)
     def _(n):
         cols = pl.ds(pl.multiple_of(n * wide_tile, wide_tile), wide_tile)
-        outrow[0, 0, :, cols] = dot(both[0], down_ref[:, cols]).astype(bf16)
-
-    far_stage(2, 0, outrow.at[0], mid.at[1])
-
-    @pl.loop(0, feat // wide_tile)
-    def _(n):
-        cols = pl.ds(pl.multiple_of(n * wide_tile, wide_tile), wide_tile)
-        mixed_rows = dot_nt(both[1], up_ref[cols, :]).astype(bf16)
-        outrow[0, 1, :, cols] = dot(cross(), mixed_rows).astype(bf16)
-
-    far_stage(2, 1, outrow.at[0], mid.at[1])
+        outrow[2, 1, :, cols] = dot(cross(), outrow[0, 1, :, cols]).astype(bf16)
+
+    far_stage(2, 1, outrow.at[2], mid.at[1])
     for stream in range(2):
         landed(2, stream, mid.at[1], small)
         mid2[1, stream] = dot(swap(False), mid[1, stream]).astype(bf16)
@@ -297,13 +359,15 @@
     back = outrow[1, 0]
     mine, weighted, named = routes[0]
     products = dot_nt(cot_ref[...], back) * mine
-    lane4 = lax.broadcasted_iota(jnp.int32, (toks, 128), 1)
-    row4 = lax.broadcasted_iota(jnp.int32, (toks, 128), 0)
-    packed = jnp.zeros((toks, 128), f32)
+    lane_of = lax.broadcasted_iota(jnp.int32, (toks, 128), 1)
+    row_of = lax.broadcasted_iota(jnp.int32, (toks, 128), 0)
+    pick_of = lax.broadcasted_iota(jnp.int32, (8, 128), 0)
+    packed = jnp.zeros((8, 128), f32)
     for j in range(picks):
-        column = jnp.sum(jnp.where(named[j], products, 0.0), axis=1, keepdims=True)
-        packed = jnp.where(lane4 == row4 * picks + j, column, packed)
-    score_box[rows_at(me, 8)] = jnp.broadcast_to(jnp.sum(packed, axis=0, keepdims=True), (8, 128))
+        score = jnp.sum(jnp.where(named[j], products, 0.0), axis=1, keepdims=True)
+        score = jnp.sum(jnp.where(lane_of == row_of, score, 0.0), axis=0, keepdims=True)
+        packed = jnp.where(pick_of == j, score, packed)
+    score_box[rows_at(me, 8)] = packed
 
     @pl.loop(1, ring)
     def _(k):
@@ -311,11 +375,7 @@
         remote(view, view, tail_send, tail_recv, wide, lax.rem(me + k, ring)).start()
 
     mixed_ref[...] = dot(weighted, back).astype(bf16)
-    ids = id_ref[...].astype(f32)
-    square = lax.broadcasted_iota(jnp.int32, (toks, toks), 0) == lax.broadcasted_iota(
-        jnp.int32, (toks, toks), 1
-    )
-    id_column = jnp.sum(jnp.where(square, ids, 0.0), axis=1, keepdims=True)
+    id_column = column(id_ref[...].astype(f32))
     samples = adv_ref.shape[1]
     match = id_column == lax.broadcasted_iota(jnp.int32, (toks, samples), 1).astype(f32)
     advantage = jnp.sum(jnp.where(match, adv_ref[...], 0.0), axis=1, keepdims=True)
@@ -327,21 +387,17 @@
     summed = score_box[pl.ds(0, 8)]
     for other in range(1, ring):
         summed = summed + score_box[pl.ds(other * 8, 8)]
-    spread = jnp.broadcast_to(summed[0:1], (toks, 128))
-    lane_pick = lax.broadcasted_iota(jnp.int32, (toks, picks), 1)
-    picked = jnp.zeros((toks, picks), f32)
-    for j in range(picks):
-        column = jnp.sum(jnp.where(lane4 == row4 * picks + j, spread, 0.0), axis=1, keepdims=True)
-        picked = jnp.where(lane_pick == j, column, picked)
-    mean_score = jnp.sum(weights * picked, axis=1, keepdims=True) / SCALE
+    picked = summed[:picks, :toks]
+    mean_score = jnp.sum(weights * picked, axis=0, keepdims=True) / SCALE
+    row_advantage = jnp.sum(jnp.where(square, advantage, 0.0), axis=0, keepdims=True)
     lgrad_ref[...] = (
-        advantage * (SCALE / total) * (picked - mean_score) * scores * (1.0 - scores)
+        row_advantage * (SCALE / total) * (picked - mean_score) * scores * (1.0 - scores)
     )
 
     for stream in range(2):
         gone(0, stream, send, big)
         gone(1, stream, mid2.at[0], small)
-        gone(2, stream, outrow.at[0], small)
+        gone(2, stream, outrow.at[2 * stream], small)
         gone(3, stream, mid2.at[1], big)
     for kind in (0, 1):
         for way in (0, 1):
@@ -361,18 +417,24 @@
         rows = mesh.shape["wide"] * SLOTS
         half = ring // 2
         vmem = pl.BlockSpec(memory_space=pltpu.VMEM)
-        hbm = pl.BlockSpec(memory_space=pl.ANY)
+        hbm = pl.BlockSpec(memory_space=pltpu.HBM)
         dma = pltpu.SemaphoreType.DMA
-        return pl.pallas_call(
+        mixed, token_grad, logit_grad = pl.pallas_call(
             functools.partial(kernel, side, ring),
             out_shape=(
                 jax.ShapeDtypeStruct((toks, feat), bf16),
                 jax.ShapeDtypeStruct((toks, feat), bf16),
-                jax.ShapeDtypeStruct(gate.shape, f32),
+                jax.ShapeDtypeStruct(gate.shape[::-1], f32),
             ),
-            in_specs=[vmem] * 6 + [hbm] * 2,
+            in_specs=[hbm] * 8,
             out_specs=[vmem] * 3,
             scratch_shapes=[
+                pltpu.VMEM((toks, feat), bf16),
+                pltpu.VMEM((toks, feat), bf16),
+                pltpu.VMEM(gate.shape[::-1], f32),
+                pltpu.VMEM(gate.shape[::-1], jnp.int32),
+                pltpu.VMEM((1, toks), jnp.int32),
+                pltpu.VMEM((1, advantages.shape[0]), f32),
                 pltpu.VMEM((feat, ff), bf16),
                 pltpu.VMEM((ff, feat), bf16),
                 pltpu.VMEM((2, rows, feat), bf16),
@@ -382,9 +444,9 @@
                 pltpu.VMEM((2, rows, ff), bf16),
                 pltpu.VMEM((2, 2, half, rows // ring, ff), bf16),
                 pltpu.VMEM((2, rows, ff), bf16),
-                pltpu.VMEM((2, 2, rows, feat), bf16),
+                pltpu.VMEM((3, 2, rows, feat), bf16),
                 pltpu.VMEM((ring * 8, 128), f32),
-                dma((2,)),
+                dma((8,)),
                 dma((4, 2)),
                 dma((4, 2)),
                 dma((2, 2, half)),
@@ -395,14 +457,15 @@
                 dma,
             ],
             compiler_params=pltpu.CompilerParams(
-                collective_id=0, has_side_effects=True, vmem_limit_bytes=40 * 1024 * 1024
+                collective_id=0, has_side_effects=True, vmem_limit_bytes=62 * 1024 * 1024
             ),
             cost_estimate=pl.CostEstimate(
                 flops=8 * rows * feat * ff, bytes_accessed=4 * feat * ff, transcendentals=0
             ),
         )(
-            tokens, cotangent, gate, groups, ids.reshape(1, toks), advantages.reshape(1, -1), up, down
+            tokens, cotangent, gate.T, groups.T, ids.reshape(1, toks), advantages.reshape(1, -1), up, down
         )
+        return mixed, token_grad, logit_grad.T
 
     in_specs = (
         P("wide", "narrow"),

time: 101 us -> 95.3 us (0.944)
  local copies, waits for them, and re-layouts: 6.63 us -> 2.64 us
  Pallas kernels: 93.8 us -> 91.8 us
    unnamed x18 -> x7, local copies, waits for them, and re-layouts: 5.98 us -> 2.64 us
    pallas_call x1, Pallas kernels: 93.8 us -> 91.8 us  [step(): pl.pallas_call(functools.partial(kernel, side, ring), out_shape=(jax.Shap...]
where the time goes in v2:
time: 95.3 us; the launch traced here: 95.1 us
  Pallas kernels  91.8 us (96%)
  local copies, waits for them, and re-layouts  2.64 us (3%)
    pallas_call x1, Pallas kernels, step(): pl.pallas_call(functools.partial(kernel, side, ring), out_shape=(jax.Shap...  91.8 us
    unnamed x7, local copies, waits for them, and re-layouts  2.64 us

profile of v2, /device:TPU:1, one launch (start us, length us, event | category | flops | bytes accessed | tf_op | source)
XLA Modules:
  0.0 95.1 jit_solution(2827734885074533973)
XLA Ops:
  0.6 91.8 %shard_map.103 = (bf16[32,512]{1,0:T(8,128)(2,1)}, bf16[32,512]{1,0:T(8,128)(2,1)}, f32[4,32]{1,0:T(4,128)}) custom-call(bf16[32,512]{1,0:T(8,128)(2,1)} %tok_hbm.1, bf16[32,512]{1,0:T(8,128)(2,1)} %cot_hbm.1, f32[4,32]{1,0:T(4,128)} %bitcast.6, s32[4,32]{1,0:T(4,128)} %bitcast.7, s32[1,32]{1,0:T(1,128)} %bitcast.8, f32[1,64]{1,0:T(1,128)} %bitcast.9, ...), custom_call_target="tpu_custom_call" | custom-call | flops 1073741824 | bytes 2097152 | tf_op jit(solution)/shard_map/pallas_call | solution.py:422
  92.4 0.0 copy-start
  92.4 1.4 %copy.14 = bf16[32,512]{1,0:T(8,128)(2,1)} copy(bf16[32,512]{1,0:T(8,128)(2,1)} %get-tuple-element.12) | data formatting | bytes 65536
  93.8 0.0 copy-done
  93.8 0.0 copy-start.1
  93.8 0.6 copy.15
  94.4 0.1 copy-done.1
  94.5 0.6 copy.16
Async XLA Ops:
  92.4 1.4 %copy-start = (bf16[32,512]{1,0:T(8,128)(2,1)S(1)}, bf16[32,512]{1,0:T(8,128)(2,1)}, u32[]{:S(2)}) copy-start(bf16[32,512]{1,0:T(8,128)(2,1)} %get-tuple-element.13) | copy-start | bytes 98308
  93.8 0.7 copy-start.1

commit v3 on v2

--- a/solution.py
+++ b/solution.py
@@ -13,6 +13,7 @@
 SCALE = 2.5
 CORES = 2
 SLOTS = 2
+SIDE_COLS = 128
 
 
 def dot(a, b):
@@ -36,20 +37,26 @@
     tok_hbm, cot_hbm, gate_hbm, group_hbm, id_hbm, adv_hbm, up_hbm, down_hbm,
     mixed_ref, tgrad_ref, lgrad_ref,
     tok_ref, cot_ref, gate_ref, group_ref, id_ref, adv_ref, up_ref, down_ref,
-    send, mid, mid2, land, part, inbox, both, outrow, score_box,
-    w_sem, st_send, st_recv, ring_send, ring_recv, ag_send, ag_recv, tail_send, tail_recv,
+    send_x, send_c, mid_x, mid_c, turn_x, turn_c, land_x, land_c, crossed, part, inbox, hidden, slopes,
+    out_y, out_g, leave_g, back_y, back_g, back_turn_y, back_turn_g, home_y, home_g, orders,
+    w_sem, st_send, st_recv, ring_send, ring_recv, ag_send, ag_recv,
 ):
     wide, me = lax.axis_index("wide"), lax.axis_index("narrow")
     my_y = lax.div(wide, side * CORES)
     my_z = lax.rem(lax.div(wide, CORES), side)
     my_c = lax.rem(wide, CORES)
     toks, feat = tok_ref.shape
-    rows = send.shape[1]
+    rows = send_x.shape[0]
     ff = up_ref.shape[1]
     big, small = rows // side, rows // (side * CORES)
     chunk = rows // ring
     half = ring // 2
-    right, left = lax.rem(me + 1, ring), lax.rem(me + ring - 1, ring)
+    all_cols = pl.ds(0, feat + SIDE_COLS)
+    halves = [pl.ds(i * (feat // 2), feat // 2) for i in range(2)]
+    def nearer(distance):
+        return half - 2 if distance == half >= 3 else distance - 1
+
+    hops = {distance - nearer(distance) for distance in range(1, half + 1)}
 
     def wide_of(y, z, c):
         return (y * side + z) * CORES + c
@@ -97,11 +104,11 @@
         greet(wide_of(spot, my_z, 0), me)
         greet(wide_of(spot, my_z, 1), me)
 
-    @pl.loop(1, ring)
-    def _(k):
-        greet(wide, lax.rem(me + k, ring))
-
-    greeted = side * CORES - 1 + (side - 1) * CORES + ring - 1
+    offsets = sorted({hop for hop in hops} | {ring - hop for hop in hops})
+    for offset in offsets:
+        greet(wide, lax.rem(me + offset, ring))
+
+    greeted = side * CORES - 1 + (side - 1) * CORES + len(offsets)
 
     for load in loads[:6]:
         load.wait()
@@ -139,9 +146,11 @@
         return mine, (mine * weighted).astype(bf16), named
 
     sources = (tok_ref, cot_ref)
-    routes = [route(stream) for stream in range(2)]
-    for stream in range(2):
-        send[stream] = dot_tn(routes[stream][0].astype(bf16), sources[stream][...]).astype(bf16)
+    routes = []
+
+    def pack(stream):
+        routes.append(route(stream))
+        sends[stream][...] = dot_tn(routes[stream][0].astype(bf16), sources[stream][...]).astype(bf16)
 
     def swap(forward):
         i = lax.broadcasted_iota(jnp.int32, (rows, rows), 0)
@@ -162,51 +171,61 @@
             device_id=(target, narrow), device_id_type=MESH,
         )
 
-    def near_stage(stage, stream, src, dst):
+    def near_stage(stage, stream, half_of, src, dst, cols):
         mine = my_near[stream]
 
         @pl.loop(1, side)
         def _(k):
             spot, target = near(stream, k)
             remote(
-                src.at[stream, rows_at(spot, big)], dst.at[stream, rows_at(mine, big)],
-                st_send.at[stage, stream], st_recv.at[stage, stream], target, me,
+                src.at[rows_at(spot, big), cols], dst.at[rows_at(mine, big), cols],
+                st_send.at[stage, stream, half_of], st_recv.at[stage, stream, half_of], target, me,
             ).start()
 
-        dst[stream, rows_at(mine, big)] = src[stream, rows_at(mine, big)]
-
-    def far_stage(stage, stream, src, dst):
+        dst[rows_at(mine, big), cols] = src[rows_at(mine, big), cols]
+
+    def far_stage(stage, stream, half_of, src, dst, cols):
         mine = my_far[stream]
 
         @pl.loop(1, side * CORES)
         def _(k):
             spot, target = far(stream, k)
             remote(
-                src.at[stream, rows_at(spot, small)], dst.at[stream, rows_at(mine, small)],
-                st_send.at[stage, stream], st_recv.at[stage, stream], target, me,
+                src.at[rows_at(spot, small), cols], dst.at[rows_at(mine, small), cols],
+                st_send.at[stage, stream, half_of], st_recv.at[stage, stream, half_of], target, me,
             ).start()
 
-        dst[stream, rows_at(mine, small)] = src[stream, rows_at(mine, small)]
-
-    def landed(stage, stream, dst, part_of):
-        view = dst.at[stream, pl.ds(0, rows - part_of)]
-        pltpu.make_async_copy(view, view, st_recv.at[stage, stream]).wait()
-
-    def gone(stage, stream, src, part_of):
-        view = src.at[stream, pl.ds(0, rows - part_of)]
-        pltpu.make_async_copy(view, view, st_send.at[stage, stream]).wait()
-
+        dst[rows_at(mine, small), cols] = src[rows_at(mine, small), cols]
+
+    def landed(stage, stream, half_of, dst, part_of, cols):
+        view = dst.at[pl.ds(0, rows - part_of), cols]
+        pltpu.make_async_copy(view, view, st_recv.at[stage, stream, half_of]).wait()
+
+    def gone(stage, stream, half_of, src, part_of, cols):
+        view = src.at[pl.ds(0, rows - part_of), cols]
+        pltpu.make_async_copy(view, view, st_send.at[stage, stream, half_of]).wait()
+
+    sends, mids, turns, lands = (send_x, send_c), (mid_x, mid_c), (turn_x, turn_c), (land_x, land_c)
+    pack(0)
     pl.semaphore_wait(barrier, greeted)
-
     for stream in range(2):
-        near_stage(0, stream, send, mid.at[0])
-    for stream in range(2):
-        landed(0, stream, mid.at[0], big)
-        mid2[0, stream] = dot(swap(True), mid[0, stream]).astype(bf16)
-        far_stage(1, stream, mid2.at[0], land)
-
-    def nearer(distance):
-        return half - 2 if distance == half >= 3 else distance - 1
+        if stream == 1:
+            pack(1)
+        for h, cols in enumerate(halves):
+            near_stage(0, stream, h, sends[stream], mids[stream], cols)
+    orders[0] = swap(True)
+    orders[1] = cross()
+    orders[2] = swap(False)
+    id_column = column(id_ref[...].astype(f32))
+    samples = adv_ref.shape[1]
+    match = id_column == lax.broadcasted_iota(jnp.int32, (toks, samples), 1).astype(f32)
+    advantage = jnp.sum(jnp.where(match, adv_ref[...], 0.0), axis=1, keepdims=True)
+    row_advantage = jnp.sum(jnp.where(square, advantage, 0.0), axis=0, keepdims=True)
+    for h, cols in enumerate(halves):
+        for stream in range(2):
+            landed(0, stream, h, mids[stream], big, cols)
+            turns[stream][:, cols] = dot(orders[0], mids[stream][:, cols]).astype(bf16)
+            far_stage(1, stream, h, turns[stream], lands[stream], cols)
 
     def longest(kind, way):
         return half if kind == way else half - 1
@@ -231,34 +250,49 @@
                 acc = acc + inbox[kind, way, distance - 1].astype(f32)
         part[kind, spot] = acc.astype(bf16)
 
-    def set_off(kind, way):
-        for distance in range(longest(kind, way), 0, -1):
-            if not any(nearer(d) == distance for d in range(1, longest(kind, way) + 1)):
+    def starts(kind, way):
+        reach = range(1, longest(kind, way) + 1)
+        return [d for d in reach if not any(nearer(other) == d for other in reach)]
+
+    def set_off(kind):
+        for way in (0, 1):
+            for distance in starts(kind, way):
                 ring_copy(kind, way, distance).start()
 
     tile = min(256, ff)
+    early = sorted({
+        (distance if way == 0 else ring - distance) % ring
+        for kind in (0, 1) for way in (0, 1) for distance in starts(kind, way)
+    })
+    late = [offset for offset in range(ring) if offset not in early]
+
+    def partial(kind, offsets_of):
+        spots = [rows_at(lax.rem(me + offset, ring), chunk) for offset in offsets_of]
+        source = crossed if kind else land_x
+        block = jnp.concatenate([source[spot] for spot in spots], axis=0)
+
+        @pl.loop(0, ff // tile)
+        def _(n):
+            cols = pl.ds(pl.multiple_of(n * tile, tile), tile)
+            out = dot_nt(block, down_ref[cols, :]) if kind else dot(block, up_ref[:, cols])
+            out = out.astype(bf16)
+            for i, spot in enumerate(spots):
+                part[kind, spot, cols] = out[i * chunk : (i + 1) * chunk]
+
     up_copy.wait()
-    landed(1, 0, land, small)
-    rows_x = land[0]
-
-    @pl.loop(0, ff // tile)
-    def _(n):
-        cols = pl.ds(pl.multiple_of(n * tile, tile), tile)
-        part[0, :, cols] = dot(rows_x, up_ref[:, cols]).astype(bf16)
-
-    set_off(0, 0)
-    set_off(0, 1)
+    for h, cols in enumerate(halves):
+        landed(1, 0, h, land_x, small, cols)
+    partial(0, early)
+    set_off(0)
     down_copy.wait()
-    landed(1, 1, land, small)
-    rows_c = dot(cross(), land[1]).astype(bf16)
-
-    @pl.loop(0, ff // tile)
-    def _(n):
-        cols = pl.ds(pl.multiple_of(n * tile, tile), tile)
-        part[1, :, cols] = dot_nt(rows_c, down_ref[cols, :]).astype(bf16)
-
-    set_off(1, 1)
-    set_off(1, 0)
+    for h, cols in enumerate(halves):
+        landed(1, 1, h, land_c, small, cols)
+    crossed[...] = dot(orders[1], land_c[...]).astype(bf16)
+    partial(1, early)
+    set_off(1)
+    if late:
+        partial(0, late)
+        partial(1, late)
     for place in range(half - 1, 0, -1):
         for kind, way in ((0, 0), (0, 1), (1, 1), (1, 0)):
             if any(nearer(d) == place for d in range(1, longest(kind, way) + 1)):
@@ -276,9 +310,11 @@
                     acc = acc + inbox[kind, way, distance - 1].astype(f32)
         return acc
 
+    both = (hidden, slopes)
+
     def pass_on(kind, way, distance):
         held = nearer(distance)
-        view = both.at[kind, rows_at(beside(1 - way, held), chunk)]
+        view = both[kind].at[rows_at(beside(1 - way, held), chunk)]
         return remote(
             view, view, ag_send.at[kind, way, distance - 1], ag_recv.at[kind, way, distance - 1],
             wide, beside(way, distance - held),
@@ -291,37 +327,40 @@
 
     def product(kind, owners):
         spots = [rows_at(owner, chunk) for owner in owners]
-        block = jnp.concatenate([both[kind, spot] for spot in spots], axis=0)
+        block = jnp.concatenate([both[kind][spot, :ff] for spot in spots], axis=0)
         out = dot(block, down_ref[...]) if kind == 0 else dot_nt(block, up_ref[...])
         out = out.astype(bf16)
         for i, (owner, spot) in enumerate(zip(owners, spots)):
-            outrow[0, kind, spot] = out[i * chunk : (i + 1) * chunk]
+            (out_y, out_g)[kind][spot, :feat] = out[i * chunk : (i + 1) * chunk]
             if kind == 0:
+                out_y[spot, feat:] = slopes[spot, ff:]
                 for core_to in range(CORES):
                     goal = owner * CORES + core_to
                     at_home = goal == my_far[0]
 
                     @pl.when(at_home)
                     def _():
-                        mid[1, 0, rows_at(goal, small)] = out[
-                            i * chunk + core_to * small : i * chunk + (core_to + 1) * small
-                        ]
+                        back_y[rows_at(goal, small)] = out_y[rows_at(goal, small)]
 
                     @pl.when(jnp.logical_not(at_home))
                     def _():
                         remote(
-                            outrow.at[0, 0, rows_at(goal, small)],
-                            mid.at[1, 0, rows_at(my_far[0], small)],
-                            st_send.at[2, 0], st_recv.at[2, 0], wide_of(owner, my_z, core_to), me,
+                            out_y.at[rows_at(goal, small)], back_y.at[rows_at(my_far[0], small)],
+                            st_send.at[2, 0, 0], st_recv.at[2, 0, 0],
+                            wide_of(owner, my_z, core_to), me,
                         ).start()
 
     pre = summed_here(0)
     sig = 1.0 / (1.0 + jnp.exp(-pre))
-    both[0, own] = (pre * sig).astype(bf16)
+    hidden_own = (pre * sig).astype(bf16)
+    hidden[own] = hidden_own
     for way in (0, 1):
         hand_on(0, way, 0)
     slope = sig * (1.0 + pre * (1.0 - sig))
-    both[1, own] = (summed_here(1) * slope).astype(bf16)
+    grad = summed_here(1)
+    slopes[own, :ff] = (grad * slope).astype(bf16)
+    score_own = jnp.sum(hidden_own.astype(f32) * grad, axis=1, keepdims=True)
+    slopes[own, ff:] = jnp.broadcast_to(score_own, (chunk, SIDE_COLS)).astype(bf16)
     for way in (1, 0):
         hand_on(1, way, 0)
     for kind in (0, 1):
@@ -342,69 +381,51 @@
                 if nearer(distance) == held
             ])
 
-    wide_tile = min(256, feat)
-
-    @pl.loop(0, feat // wide_tile)
-    def _(n):
-        cols = pl.ds(pl.multiple_of(n * wide_tile, wide_tile), wide_tile)
-        outrow[2, 1, :, cols] = dot(cross(), outrow[0, 1, :, cols]).astype(bf16)
-
-    far_stage(2, 1, outrow.at[2], mid.at[1])
-    for stream in range(2):
-        landed(2, stream, mid.at[1], small)
-        mid2[1, stream] = dot(swap(False), mid[1, stream]).astype(bf16)
-        near_stage(3, stream, mid2.at[1], outrow.at[1])
-
-    landed(3, 0, outrow.at[1], big)
-    back = outrow[1, 0]
+    for h, cols in enumerate(halves):
+        leave_g[:, cols] = dot(orders[1], out_g[:, cols]).astype(bf16)
+        far_stage(2, 1, h, leave_g, back_g, cols)
+    landed(2, 0, 0, back_y, small, all_cols)
+    back_turn_y[...] = dot(orders[2], back_y[...]).astype(bf16)
+    near_stage(3, 0, 0, back_turn_y, home_y, all_cols)
+    for h, cols in enumerate(halves):
+        landed(2, 1, h, back_g, small, cols)
+        back_turn_g[:, cols] = dot(orders[2], back_g[:, cols]).astype(bf16)
+        near_stage(3, 1, h, back_turn_g, home_g, cols)
+
+    landed(3, 0, 0, home_y, big, all_cols)
     mine, weighted, named = routes[0]
-    products = dot_nt(cot_ref[...], back) * mine
-    lane_of = lax.broadcasted_iota(jnp.int32, (toks, 128), 1)
-    row_of = lax.broadcasted_iota(jnp.int32, (toks, 128), 0)
-    pick_of = lax.broadcasted_iota(jnp.int32, (8, 128), 0)
-    packed = jnp.zeros((8, 128), f32)
+    mixed_ref[...] = dot(weighted, home_y[:, :feat]).astype(bf16)
+    scores_back = home_y[:, feat:]
+    lane_of = lax.broadcasted_iota(jnp.int32, (toks, SIDE_COLS), 1)
+    row_of = lax.broadcasted_iota(jnp.int32, (toks, SIDE_COLS), 0)
+    pick_of = lax.broadcasted_iota(jnp.int32, (picks, SIDE_COLS), 0)
+    packed = jnp.zeros((picks, SIDE_COLS), f32)
     for j in range(picks):
-        score = jnp.sum(jnp.where(named[j], products, 0.0), axis=1, keepdims=True)
+        score = dot(jnp.where(named[j], mine, 0.0).astype(bf16), scores_back)
         score = jnp.sum(jnp.where(lane_of == row_of, score, 0.0), axis=0, keepdims=True)
         packed = jnp.where(pick_of == j, score, packed)
-    score_box[rows_at(me, 8)] = packed
-
-    @pl.loop(1, ring)
-    def _(k):
-        view = score_box.at[rows_at(me, 8)]
-        remote(view, view, tail_send, tail_recv, wide, lax.rem(me + k, ring)).start()
-
-    mixed_ref[...] = dot(weighted, back).astype(bf16)
-    id_column = column(id_ref[...].astype(f32))
-    samples = adv_ref.shape[1]
-    match = id_column == lax.broadcasted_iota(jnp.int32, (toks, samples), 1).astype(f32)
-    advantage = jnp.sum(jnp.where(match, adv_ref[...], 0.0), axis=1, keepdims=True)
-    landed(3, 1, outrow.at[1], big)
-    tgrad_ref[...] = (advantage * dot(routes[1][1], outrow[1, 1])).astype(bf16)
-
-    tail_view = score_box.at[pl.ds(0, (ring - 1) * 8)]
-    pltpu.make_async_copy(tail_view, tail_view, tail_recv).wait()
-    summed = score_box[pl.ds(0, 8)]
-    for other in range(1, ring):
-        summed = summed + score_box[pl.ds(other * 8, 8)]
-    picked = summed[:picks, :toks]
+    picked = packed[:, :toks]
     mean_score = jnp.sum(weights * picked, axis=0, keepdims=True) / SCALE
-    row_advantage = jnp.sum(jnp.where(square, advantage, 0.0), axis=0, keepdims=True)
     lgrad_ref[...] = (
         row_advantage * (SCALE / total) * (picked - mean_score) * scores * (1.0 - scores)
     )
-
-    for stream in range(2):
-        gone(0, stream, send, big)
-        gone(1, stream, mid2.at[0], small)
-        gone(2, stream, outrow.at[2 * stream], small)
-        gone(3, stream, mid2.at[1], big)
+    for h, cols in enumerate(halves):
+        landed(3, 1, h, home_g, big, cols)
+    tgrad_ref[...] = (advantage * dot(routes[1][1], home_g[...])).astype(bf16)
+
+    for h, cols in enumerate(halves):
+        for stream in range(2):
+            gone(0, stream, h, sends[stream], big, cols)
+            gone(1, stream, h, turns[stream], small, cols)
+        gone(2, 1, h, leave_g, small, cols)
+        gone(3, 1, h, back_turn_g, big, cols)
+    gone(2, 0, 0, out_y, small, all_cols)
+    gone(3, 0, 0, back_turn_y, big, all_cols)
     for kind in (0, 1):
         for way in (0, 1):
             for distance in range(1, longest(kind, way) + 1):
                 ring_copy(kind, way, distance).wait_send()
                 pass_on(kind, way, distance).wait_send()
-    pltpu.make_async_copy(tail_view, tail_view, tail_send).wait()
 
 
 def solution(mesh):
@@ -422,9 +443,9 @@
         mixed, token_grad, logit_grad = pl.pallas_call(
             functools.partial(kernel, side, ring),
             out_shape=(
-                jax.ShapeDtypeStruct((toks, feat), bf16),
-                jax.ShapeDtypeStruct((toks, feat), bf16),
-                jax.ShapeDtypeStruct(gate.shape[::-1], f32),
+                pltpu.VMEM((toks, feat), bf16),
+                pltpu.VMEM((toks, feat), bf16),
+                pltpu.VMEM(gate.shape[::-1], f32),
             ),
             in_specs=[hbm] * 8,
             out_specs=[vmem] * 3,
@@ -437,24 +458,22 @@
                 pltpu.VMEM((1, advantages.shape[0]), f32),
                 pltpu.VMEM((feat, ff), bf16),
                 pltpu.VMEM((ff, feat), bf16),
-                pltpu.VMEM((2, rows, feat), bf16),
-                pltpu.VMEM((2, 2, rows, feat), bf16),
-                pltpu.VMEM((2, 2, rows, feat), bf16),
-                pltpu.VMEM((2, rows, feat), bf16),
+                *[pltpu.VMEM((rows, feat), bf16)] * 9,
                 pltpu.VMEM((2, rows, ff), bf16),
                 pltpu.VMEM((2, 2, half, rows // ring, ff), bf16),
-                pltpu.VMEM((2, rows, ff), bf16),
-                pltpu.VMEM((3, 2, rows, feat), bf16),
-                pltpu.VMEM((ring * 8, 128), f32),
+                pltpu.VMEM((rows, ff), bf16),
+                pltpu.VMEM((rows, ff + SIDE_COLS), bf16),
+                *[pltpu.VMEM((rows, feat + extra), bf16) for extra in (
+                    SIDE_COLS, 0, 0, SIDE_COLS, 0, SIDE_COLS, 0, SIDE_COLS, 0,
+                )],
+                pltpu.VMEM((3, rows, rows), bf16),
                 dma((8,)),
-                dma((4, 2)),
-                dma((4, 2)),
+                dma((4, 2, 2)),
+                dma((4, 2, 2)),
                 dma((2, 2, half)),
                 dma((2, 2, half)),
                 dma((2, 2, half)),
                 dma((2, 2, half)),
-                dma,
-                dma,
             ],
             compiler_params=pltpu.CompilerParams(
                 collective_id=0, has_side_effects=True, vmem_limit_bytes=62 * 1024 * 1024

time: 95.3 us -> 90.2 us (0.946)
  Pallas kernels: 91.8 us -> 87.2 us
    pallas_call x1, Pallas kernels: 91.8 us -> 87.2 us  [step(): pl.pallas_call(functools.partial(kernel, side, ring), out_shape=(pltpu.VM...]
    unnamed x7 -> x3, local copies, waits for them, and re-layouts: 2.64 us -> 1.81 us
where the time goes in v3:
time: 90.2 us; the launch traced here: 89.6 us
  Pallas kernels  87.2 us (97%)
  local copies, waits for them, and re-layouts  1.81 us (2%)
    pallas_call x1, Pallas kernels, step(): pl.pallas_call(functools.partial(kernel, side, ring), out_shape=(pltpu.VM...  87.2 us
    unnamed x3, local copies, waits for them, and re-layouts  1.81 us

profile of v3, /device:TPU:1, one launch (start us, length us, event | category | flops | bytes accessed | tf_op | source)
XLA Modules:
  0.0 89.6 jit_solution(1088557908114097674)
XLA Ops:
  0.6 87.2 %shard_map.103 = (bf16[32,512]{1,0:T(8,128)(2,1)S(1)}, bf16[32,512]{1,0:T(8,128)(2,1)S(1)}, f32[4,32]{1,0:T(4,128)S(1)}) custom-call(bf16[32,512]{1,0:T(8,128)(2,1)} %tok_hbm.1, bf16[32,512]{1,0:T(8,128)(2,1)} %cot_hbm.1, f32[4,32]{1,0:T(4,128)} %bitcast.6, s32[4,32]{1,0:T(4,128)} %bitcast.7, s32[1,32]{1,0:T(1,128)} %bitcast.8, f32[1,64]{1,0:T(1,128)} %bitcast.9, ...), custom_call_target="tpu_custom_call" | custom-call | flops 1073741824 | bytes 2097152 | tf_op jit(solution)/shard_map/pallas_call | solution.py:443
  87.8 0.6 copy.14
  88.4 0.6 copy.16
  89.0 0.6 copy.15

commit v4 on v3

--- a/solution.py
+++ b/solution.py
@@ -52,7 +52,7 @@
     chunk = rows // ring
     half = ring // 2
     all_cols = pl.ds(0, feat + SIDE_COLS)
-    halves = [pl.ds(i * (feat // 2), feat // 2) for i in range(2)]
+    halves = [pl.ds(i * (feat // 4), feat // 4) for i in range(4)]
     def nearer(distance):
         return half - 2 if distance == half >= 3 else distance - 1
 
@@ -171,12 +171,16 @@
             device_id=(target, narrow), device_id_type=MESH,
         )
 
+    def farthest_first(size, k):
+        hop = lax.div(k + 1, 2)
+        return size // 2 + hop * (1 - 2 * lax.rem(k, 2))
+
     def near_stage(stage, stream, half_of, src, dst, cols):
         mine = my_near[stream]
 
-        @pl.loop(1, side)
+        @pl.loop(0, side - 1)
         def _(k):
-            spot, target = near(stream, k)
+            spot, target = near(stream, farthest_first(side, k))
             remote(
                 src.at[rows_at(spot, big), cols], dst.at[rows_at(mine, big), cols],
                 st_send.at[stage, stream, half_of], st_recv.at[stage, stream, half_of], target, me,
@@ -187,9 +191,9 @@
     def far_stage(stage, stream, half_of, src, dst, cols):
         mine = my_far[stream]
 
-        @pl.loop(1, side * CORES)
+        @pl.loop(0, side * CORES - 1)
         def _(k):
-            spot, target = far(stream, k)
+            spot, target = far(stream, farthest_first(side * CORES, k))
             remote(
                 src.at[rows_at(spot, small), cols], dst.at[rows_at(mine, small), cols],
                 st_send.at[stage, stream, half_of], st_recv.at[stage, stream, half_of], target, me,
@@ -468,8 +472,8 @@
                 )],
                 pltpu.VMEM((3, rows, rows), bf16),
                 dma((8,)),
-                dma((4, 2, 2)),
-                dma((4, 2, 2)),
+                dma((4, 2, 4)),
+                dma((4, 2, 4)),
                 dma((2, 2, half)),
                 dma((2, 2, half)),
                 dma((2, 2, half)),

time: 90.2 us -> 89.2 us (0.989)
  Pallas kernels: 87.2 us -> 85.9 us
    pallas_call x1, Pallas kernels: 87.2 us -> 85.9 us  [step(): pl.pallas_call(functools.partial(kernel, side, ring), out_shape=(pltpu.VM...]
where the time goes in v4:
time: 89.2 us; the launch traced here: 88.3 us
  Pallas kernels  85.9 us (96%)
  local copies, waits for them, and re-layouts  1.81 us (2%)
    pallas_call x1, Pallas kernels, step(): pl.pallas_call(functools.partial(kernel, side, ring), out_shape=(pltpu.VM...  85.9 us
    unnamed x3, local copies, waits for them, and re-layouts  1.81 us

profile of v4, /device:TPU:1, one launch (start us, length us, event | category | flops | bytes accessed | tf_op | source)
XLA Modules:
  0.0 88.3 jit_solution(17364927338064903760)
XLA Ops:
  0.6 85.9 %shard_map.103 = (bf16[32,512]{1,0:T(8,128)(2,1)S(1)}, bf16[32,512]{1,0:T(8,128)(2,1)S(1)}, f32[4,32]{1,0:T(4,128)S(1)}) custom-call(bf16[32,512]{1,0:T(8,128)(2,1)} %tok_hbm.1, bf16[32,512]{1,0:T(8,128)(2,1)} %cot_hbm.1, f32[4,32]{1,0:T(4,128)} %bitcast.6, s32[4,32]{1,0:T(4,128)} %bitcast.7, s32[1,32]{1,0:T(1,128)} %bitcast.8, f32[1,64]{1,0:T(1,128)} %bitcast.9, ...), custom_call_target="tpu_custom_call" | custom-call | flops 1073741824 | bytes 2097152 | tf_op jit(solution)/shard_map/pallas_call | solution.py:447
  86.5 0.6 copy.14
  87.2 0.6 copy.16
  87.7 0.6 copy.15
